TPU v7x, 256 devices: a whole 4x4x8 slice. The times are simulated.
256 devices in a mesh: group: 32 (over x_lo, z, core), tensor: 8 (over x_hi, y).
Axes of the slice: x: 4 (x_hi: 2, x_lo: 2; x = x_hi * 2 + x_lo), y: 4, z: 8, core: 2. Of those that a mesh axis runs over, the one named last changes fastest.
Arguments:
- ssm_input: bfloat16 [16384, 16384], P('group', 'tensor'), may hold values from -6 to 6
- gate_input: bfloat16 [16384, 16384], P('group', 'tensor'), may hold values from -12 to 12
- step_sizes: float32 [256, 16384], P('tensor', 'group'), may hold values from 0.25 to 102
- decay_rates: float32 [256], P('tensor'), as said below
- state_write: bfloat16 [16384, 2048], P('group', 'tensor'), may hold values from -0.25 to 0.25
- state_read: bfloat16 [16384, 2048], P('group', 'tensor'), may hold values from -0.375 to 0.375
- norm_gain: float32 [16384], P('tensor'), may hold values from 0.1 to 1.9
- queries: bfloat16 [16384, 8192], P('group', 'tensor'), may hold values from -6 to 6
- suffix_keys: bfloat16 [16384, 1024], P('group', 'tensor'), may hold values from -6 to 6
- suffix_values: bfloat16 [16384, 1024], P('group', 'tensor'), may hold values from -6 to 6
- held_state: bfloat16 [32, 256, 64, 256], P('group', 'tensor'), may hold values from -6 to 6
- held_cache: bfloat16 [32, 2, 512, 1024], P('group', None, None, 'tensor'), may hold values from -6 to 6
- prefix_ids: int32 [32], replicated, may hold values from 0 to 31
- prefix_lengths: int32 [32], replicated, may hold values from 1 to 512, as said below
- holder_slots: int32 [32], replicated, may hold values from 0 to 31, each once
- new_holders: int32 [32], replicated, may hold values from 0 to 31, each once
Outputs:
- ssm_out: bfloat16 [16384, 16384], P('group', 'tensor')
- attn_out: bfloat16 [16384, 8192], P('group', 'tensor')
- stored_state: bfloat16 [32, 256, 64, 256], P('group', 'tensor')
Inputs may be any that keep to these rules, and one draw needn't show every extreme that they name: `prefix_lengths`: some prefix has exactly 512 tokens. `holder_slots`: each prefix lives in its own slot. `new_holders`: each slot keeps the state of exactly one request. `decay_rates`: Positive.
All inputs are finite; a program needn't handle non-finite values.
Results may differ from a plain program's by a relative error of at most 0.005.
Values may be sent and summed in bfloat16 or wider, within the bound.
A program may use at most 256 MiB of HBM per device.

v0:
```python
import jax
import jax.numpy as jnp
from jax import lax
from jax.experimental import pallas as pl
from jax.experimental.pallas import tpu as pltpu
from jax.sharding import PartitionSpec as P

MHEADS = 256
MDIM = 64
STATE = 256
HDIM = 128
BLOCK = 256
ROWS = 512
LP = 512
SLOTS = 32
HEADS = 32
PAIRS = HEADS // 2
QH = 8
RANKS = 8
PIECE = LP // SLOTS
EPSILON = 1e-05
LOW = -1e30
MESH = pl.DeviceIdType.MESH
F32 = jnp.float32
BF16 = jnp.bfloat16


def dot(a, b):
    return jnp.dot(a, b, preferred_element_type=F32)


def dot_nt(a, b):
    return lax.dot_general(a, b, (((1,), (1,)), ((), ())), preferred_element_type=F32)


def kernel(
    ids,
    lengths,
    holders,
    sources,
    rates,
    steps,
    gain,
    x_hbm,
    gate_hbm,
    write_hbm,
    read_hbm,
    q_hbm,
    sk_hbm,
    sv_hbm,
    held,
    cache,
    ssm_out,
    attn_out,
    stored,
    x_v,
    gate_v,
    write_v,
    read_v,
    q_v,
    sk_v,
    sv_v,
    cum_v,
    scale_v,
    fade_v,
    gram_v,
    entry_v,
    y_v,
    decay_v,
    held_a,
    cache_a,
    local_mine,
    local_a,
    total_mine,
    total_a,
    held_p,
    held_b,
    cache_p,
    cache_b,
    final_p,
    attn_v,
    norm_v,
    square_mine,
    square_a,
    in_sem,
    out_sem,
    own_sem,
    send_sem,
    recv_sem,
):
    me = lax.axis_index("group")
    rank = lax.axis_index("tensor")

    loads = []
    for n, (src, dst) in enumerate(
        (
            (x_hbm, x_v),
            (write_hbm, write_v),
            (read_hbm, read_v),
            (q_hbm, q_v),
            (sk_hbm, sk_v),
            (sv_hbm, sv_v),
            (gate_hbm, gate_v),
        )
    ):
        loads.append(pltpu.make_async_copy(src, dst, in_sem.at[n]))
        loads[-1].start()

    barrier = pltpu.get_barrier_semaphore()

    def greet_member(k, carry):
        pl.semaphore_signal(
            barrier, inc=1, device_id={"group": lax.rem(me + k, SLOTS)}, device_id_type=MESH
        )
        return carry

    def greet_rank(k, carry):
        pl.semaphore_signal(
            barrier, inc=1, device_id={"tensor": lax.rem(rank + k, RANKS)}, device_id_type=MESH
        )
        return carry

    lax.fori_loop(1, SLOTS, greet_member, 0)
    lax.fori_loop(1, RANKS, greet_rank, 0)

    def head_logs(h, carry):
        row = pl.ds(h, 1)
        cum_v[row, :] = steps[row, :] * -rates[h]
        return carry

    lax.fori_loop(0, HEADS, head_logs, 0)
    at_u = lax.broadcasted_iota(jnp.int32, (BLOCK, BLOCK), 0)
    at_t = lax.broadcasted_iota(jnp.int32, (BLOCK, BLOCK), 1)
    upper = (at_u <= at_t).astype(F32)
    ends = []
    for b in range(2):
        cols = slice(b * BLOCK, (b + 1) * BLOCK)
        cum = jnp.dot(
            cum_v[:, cols], upper, preferred_element_type=F32, precision=lax.Precision.HIGHEST
        )
        end = cum[:, BLOCK - 1 : BLOCK]
        cum_v[:, cols] = cum
        scale_v[:, cols] = jnp.exp(end - cum) * steps[:, cols]
        ends.append(end)
    fade_v[...] = jnp.broadcast_to(jnp.exp(ends[1]), (HEADS, STATE))
    total_mine[...] = jnp.broadcast_to(jnp.exp(ends[0] + ends[1]), (HEADS, 128)).reshape(
        HEADS, 1, 128
    )

    pl.semaphore_wait(barrier, SLOTS - 1 + RANKS - 1)

    def to_member(p, src, dst, n):
        return pltpu.make_async_remote_copy(
            src_ref=src,
            dst_ref=dst,
            send_sem=send_sem.at[n],
            recv_sem=recv_sem.at[n],
            device_id={"group": p},
            device_id_type=MESH,
        )

    def arrived(buf, n, count=SLOTS - 1):
        part = buf.at[pl.ds(0, count)]
        pltpu.make_async_copy(part, part, recv_sem.at[n]).wait()

    def sent(buf, n, count=SLOTS - 1):
        part = buf.at[pl.ds(0, count)]
        pltpu.make_async_copy(part, part, send_sem.at[n]).wait()

    def cache_rows(p):
        return cache.at[0, :, pl.ds(pl.multiple_of(p * PIECE, PIECE), PIECE), :]

    def spread_cache(k, carry):
        p = lax.rem(me + k, SLOTS)
        to_member(p, cache_rows(p), cache_a.at[me], 0).start()
        return carry

    def spread_held(k, carry):
        p = lax.rem(me + k, SLOTS)
        to_member(p, held.at[0, p], held_a.at[me], 1).start()
        return carry

    lax.fori_loop(1, SLOTS, spread_cache, 0)
    lax.fori_loop(1, SLOTS, spread_held, 0)
    own_cache = pltpu.make_async_copy(cache_rows(me), cache_a.at[me], own_sem.at[0])
    own_held = pltpu.make_async_copy(held.at[0, me], held_a.at[me], own_sem.at[1])
    own_cache.start()
    own_held.start()

    loads[0].wait()
    loads[1].wait()
    first_row = lax.broadcasted_iota(jnp.int32, (2 * MDIM, 1), 0) < MDIM

    def local_state(j, carry):
        a, b = pl.ds(2 * j, 1), pl.ds(2 * j + 1, 1)
        pair = pl.ds(pl.multiple_of(j * 128, 128), 128)
        turned = jnp.transpose(x_v[:, pair].astype(F32))
        scaled = (turned * jnp.where(first_row, scale_v[a, :], scale_v[b, :])).astype(BF16)
        entry = dot(scaled[:, :BLOCK], write_v[:BLOCK, :])
        later = dot(scaled[:, BLOCK:], write_v[BLOCK:, :])
        entry_v[j] = entry.astype(BF16)
        fade = jnp.where(first_row, fade_v[a, :], fade_v[b, :])
        local_mine[pl.ds(2 * j, 2)] = (
            (fade * entry + later).astype(BF16).reshape(2, MDIM, STATE)
        )
        return carry

    lax.fori_loop(0, PAIRS, local_state, 0)

    def spread_local(k, carry):
        p = lax.rem(me + k, SLOTS)
        to_member(p, local_mine.at[p], local_a.at[me], 2).start()
        to_member(p, total_mine.at[p], total_a.at[me], 3).start()
        return carry

    lax.fori_loop(1, SLOTS, spread_local, 0)
    local_a[me] = local_mine[me]
    total_a[me] = total_mine[me]

    own_cache.wait()
    arrived(cache_a, 0)

    def pick_cache(r, carry):
        cache_p[r] = cache_a[holders[ids[r]]]
        return carry

    lax.fori_loop(0, SLOTS, pick_cache, 0)

    def gather_cache(k, carry):
        p = lax.rem(me + k, SLOTS)
        to_member(p, cache_p.at[p], cache_b.at[me], 4).start()
        return carry

    lax.fori_loop(1, SLOTS, gather_cache, 0)
    cache_b[me] = cache_p[me]

    loads[2].wait()
    for b in range(2):
        rows = slice(b * BLOCK, (b + 1) * BLOCK)
        gram_v[b] = dot_nt(read_v[rows, :], write_v[rows, :])
    first_lane = lax.broadcasted_iota(jnp.int32, (1, 128), 1) < MDIM
    causal = at_u >= at_t

    def inner_values(j, carry):
        pair = pl.ds(pl.multiple_of(j * 128, 128), 128)
        xs = x_v[:, pair]
        zero = jnp.zeros_like(xs)
        halves = (jnp.where(first_lane, xs, zero), jnp.where(first_lane, zero, xs))
        tall = []
        values = [None, None]
        for i in range(2):
            row = pl.ds(2 * j + i, 1)
            cum = cum_v[row, :]
            column = jnp.transpose(jnp.broadcast_to(cum, (128, ROWS)))
            tall.append(column)
            for b in range(2):
                rows = slice(b * BLOCK, (b + 1) * BLOCK)
                left = column[rows, :]
                gap = jnp.concatenate([left, left], axis=1) - cum[:, rows]
                decays = jnp.exp(jnp.where(causal, gap, LOW))
                weights = (gram_v[b] * decays * steps[row, rows]).astype(BF16)
                part = dot(weights, halves[i][rows, :])
                values[b] = part if values[b] is None else values[b] + part
        column = jnp.where(first_lane, tall[0], tall[1])
        early, late = column[:BLOCK, :], column[BLOCK:, :]
        entered = dot_nt(read_v[BLOCK:, :], entry_v[j])
        decay_v[j, :BLOCK, :] = jnp.exp(early)
        decay_v[j, BLOCK:, :] = jnp.exp(late + early[BLOCK - 1 : BLOCK, :])
        y_v[j, :BLOCK, :] = values[0]
        y_v[j, BLOCK:, :] = values[1] + jnp.exp(late) * entered
        return carry

    lax.fori_loop(0, PAIRS, inner_values, 0)

    own_held.wait()
    arrived(held_a, 1)

    def pick_held(r, carry):
        held_p[r] = held_a[holders[ids[r]]]
        return carry

    lax.fori_loop(0, SLOTS, pick_held, 0)

    def gather_held(k, carry):
        p = lax.rem(me + k, SLOTS)
        to_member(p, held_p.at[p], held_b.at[me], 5).start()
        return carry

    lax.fori_loop(1, SLOTS, gather_held, 0)
    held_b[me] = held_p[me]

    for n in (3, 4, 5):
        loads[n].wait()
    arrived(cache_b, 4)
    length = lengths[ids[me]]
    prefix_allowed = lax.broadcasted_iota(jnp.int32, (1, LP), 1) < length
    score_scale = HDIM ** (-0.5)

    def attend(h, carry):
        head = pl.ds(pl.multiple_of(h * HDIM, HDIM), HDIM)
        prefix_keys = cache_b[:, 0].reshape(LP, HDIM)
        prefix_values = cache_b[:, 1].reshape(LP, HDIM)
        for b in range(2):
            rows = slice(b * BLOCK, (b + 1) * BLOCK)
            width = (b + 1) * BLOCK
            q = q_v[rows, head]
            prefix = dot_nt(q, prefix_keys) * score_scale
            prefix = jnp.where(prefix_allowed, prefix, LOW)
            own = dot_nt(q, sk_v[:width, :]) * score_scale
            t = lax.broadcasted_iota(jnp.int32, (BLOCK, width), 0) + b * BLOCK
            u = lax.broadcasted_iota(jnp.int32, (BLOCK, width), 1)
            own = jnp.where(u <= t, own, LOW)
            highest = jnp.maximum(
                jnp.max(prefix, axis=1, keepdims=True), jnp.max(own, axis=1, keepdims=True)
            )
            prefix = jnp.exp(prefix - highest)
            own = jnp.exp(own - highest)
            totals = jnp.sum(prefix, axis=1, keepdims=True) + jnp.sum(own, axis=1, keepdims=True)
            mixed = dot(prefix.astype(BF16), prefix_values) + dot(own.astype(BF16), sv_v[:width, :])
            attn_v[rows, head] = (mixed / totals).astype(BF16)
        return carry

    lax.fori_loop(0, QH, attend, 0)
    attn_store = pltpu.make_async_copy(attn_v, attn_out, out_sem.at[0])
    attn_store.start()

    arrived(local_a, 2)
    arrived(total_a, 3)

    def pick_final(d, carry):
        r = sources[d]
        start = held_a[holders[ids[r]]].astype(F32)
        fade = total_a[r]
        fade = jnp.concatenate([fade, fade], axis=1)
        final_p[d] = (start * fade + local_a[r].astype(F32)).astype(BF16)
        return carry

    lax.fori_loop(0, SLOTS, pick_final, 0)

    def store_final(k, carry):
        p = lax.rem(me + k, SLOTS)
        to_member(p, final_p.at[p], stored.at[0, me], 6).start()
        return carry

    lax.fori_loop(1, SLOTS, store_final, 0)
    own_final = pltpu.make_async_copy(final_p.at[me], stored.at[0, me], own_sem.at[2])
    own_final.start()

    loads[6].wait()
    arrived(held_b, 5)

    def gate_values(j, squares):
        pair = pl.ds(pl.multiple_of(j * 128, 128), 128)
        start = held_b[pl.ds(2 * j, 2)].reshape(2 * MDIM, STATE)
        values = y_v[j] + decay_v[j] * dot_nt(read_v[...], start)
        gate = gate_v[:, pair].astype(F32)
        values = values * (gate / (1.0 + jnp.exp(-gate)))
        y_v[j] = values
        return squares + values * values

    squares = lax.fori_loop(0, PAIRS, gate_values, jnp.zeros((ROWS, 128), F32))
    square_mine[...] = jnp.sum(jnp.transpose(squares), axis=0, keepdims=True)

    def send_squares(k, carry):
        pltpu.make_async_remote_copy(
            src_ref=square_mine,
            dst_ref=square_a.at[rank],
            send_sem=send_sem.at[7],
            recv_sem=recv_sem.at[7],
            device_id={"tensor": lax.rem(rank + k, RANKS)},
            device_id_type=MESH,
        ).start()
        return carry

    lax.fori_loop(1, RANKS, send_squares, 0)
    square_a[rank] = square_mine[...]
    arrived(square_a, 7, RANKS - 1)
    mean_square = jnp.sum(square_a[...], axis=0) / (MHEADS * MDIM)
    inverse = lax.rsqrt(mean_square + EPSILON)
    inverse = jnp.transpose(jnp.broadcast_to(inverse, (128, ROWS)))

    def norm(j, carry):
        pair = pl.ds(pl.multiple_of(j * 128, 128), 128)
        norm_v[:, pair] = (y_v[j] * inverse * gain[pl.ds(j, 1), :]).astype(BF16)
        return carry

    lax.fori_loop(0, PAIRS, norm, 0)
    norm_store = pltpu.make_async_copy(norm_v, ssm_out, out_sem.at[1])
    norm_store.start()

    attn_store.wait()
    norm_store.wait()
    own_final.wait()
    sent(cache_a, 0)
    sent(held_a, 1)
    sent(local_a, 2)
    sent(total_a, 3)
    sent(cache_b, 4)
    sent(held_b, 5)
    sent(final_p, 6)
    sent(square_a, 7, RANKS - 1)
    part = stored.at[0, pl.ds(0, SLOTS - 1)]
    pltpu.make_async_copy(part, part, recv_sem.at[6]).wait()


def local(
    ssm_input,
    gate_input,
    step_sizes,
    decay_rates,
    state_write,
    state_read,
    norm_gain,
    queries,
    suffix_keys,
    suffix_values,
    held_state,
    held_cache,
    prefix_ids,
    prefix_lengths,
    holder_slots,
    new_holders,
):
    slots = jnp.arange(SLOTS, dtype=jnp.int32)
    sources = jnp.sum(jnp.where(new_holders[None, :] == slots[:, None], slots[None, :], 0), 1)
    smem = pl.BlockSpec(memory_space=pltpu.SMEM)
    vmem = pl.BlockSpec(memory_space=pltpu.VMEM)
    anywhere = pl.BlockSpec(memory_space=pl.ANY)
    state = (SLOTS, MDIM, STATE)
    cache = (SLOTS, 2, PIECE, HDIM)
    return pl.pallas_call(
        kernel,
        out_shape=(
            jax.ShapeDtypeStruct((ROWS, HEADS * MDIM), BF16),
            jax.ShapeDtypeStruct((ROWS, QH * HDIM), BF16),
            jax.ShapeDtypeStruct((1,) + state, BF16),
        ),
        in_specs=[smem] * 5 + [vmem] * 2 + [anywhere] * 9,
        out_specs=(anywhere,) * 3,
        scratch_shapes=[
            pltpu.VMEM((ROWS, HEADS * MDIM), BF16),
            pltpu.VMEM((ROWS, HEADS * MDIM), BF16),
            pltpu.VMEM((ROWS, STATE), BF16),
            pltpu.VMEM((ROWS, STATE), BF16),
            pltpu.VMEM((ROWS, QH * HDIM), BF16),
            pltpu.VMEM((ROWS, HDIM), BF16),
            pltpu.VMEM((ROWS, HDIM), BF16),
            pltpu.VMEM((HEADS, ROWS), F32),
            pltpu.VMEM((HEADS, ROWS), F32),
            pltpu.VMEM((HEADS, STATE), F32),
            pltpu.VMEM((2, BLOCK, BLOCK), F32),
            pltpu.VMEM((PAIRS, 2 * MDIM, STATE), BF16),
            pltpu.VMEM((PAIRS, ROWS, 128), F32),
            pltpu.VMEM((PAIRS, ROWS, 128), F32),
            pltpu.VMEM(state, BF16),
            pltpu.VMEM(cache, BF16),
            pltpu.VMEM(state, BF16),
            pltpu.VMEM(state, BF16),
            pltpu.VMEM((HEADS, 1, 128), F32),
            pltpu.VMEM((SLOTS, 1, 128), F32),
            pltpu.VMEM(state, BF16),
            pltpu.VMEM(state, BF16),
            pltpu.VMEM(cache, BF16),
            pltpu.VMEM(cache, BF16),
            pltpu.VMEM(state, BF16),
            pltpu.VMEM((ROWS, QH * HDIM), BF16),
            pltpu.VMEM((ROWS, HEADS * MDIM), BF16),
            pltpu.VMEM((1, ROWS), F32),
            pltpu.VMEM((RANKS, 1, ROWS), F32),
            pltpu.SemaphoreType.DMA((7,)),
            pltpu.SemaphoreType.DMA((2,)),
            pltpu.SemaphoreType.DMA((3,)),
            pltpu.SemaphoreType.DMA((8,)),
            pltpu.SemaphoreType.DMA((8,)),
        ],
        compiler_params=pltpu.CompilerParams(
            collective_id=0, has_side_effects=True, vmem_limit_bytes=52 * 2**20
        ),
        name="layer_pair",
    )(
        prefix_ids,
        prefix_lengths,
        holder_slots,
        sources,
        decay_rates,
        step_sizes,
        norm_gain.reshape(PAIRS, 128),
        ssm_input,
        gate_input,
        state_write,
        state_read,
        queries,
        suffix_keys,
        suffix_values,
        held_state,
        held_cache,
    )


def solution(mesh):
    return jax.shard_map(
        local,
        mesh=mesh,
        in_specs=(
            P("group", "tensor"),
            P("group", "tensor"),
            P("tensor", "group"),
            P("tensor"),
            P("group", "tensor"),
            P("group", "tensor"),
            P("tensor"),
            P("group", "tensor"),
            P("group", "tensor"),
            P("group", "tensor"),
            P("group", "tensor", None, None),
            P("group", None, None, "tensor"),
            P(),
            P(),
            P(),
            P(),
        ),
        out_specs=(P("group", "tensor"), P("group", "tensor"), P("group", "tensor", None, None)),
        check_vma=False,
    )
```

profile of v0, /device:TPU:1, one launch (start us, length us, event | category | flops | bytes accessed | tf_op | source)
XLA Modules:
  0.0 132.6 jit_solution(4629780888740561578)
XLA Ops:
  0.6 0.8 select_reduce_fusion.sources
  1.4 0.0 copy-start
  1.4 0.9 copy-done
  2.4 0.0 copy-start.1
  2.4 0.9 copy-done.1
  3.3 0.9 copy-done.2
  4.3 0.0 copy-start.3
  4.3 0.9 copy-done.3
  5.2 0.0 copy-start.4
  5.2 0.9 copy-done.4
  6.1 0.8 copy-done.5
  6.9 0.7 copy-done.6
  7.6 0.7 copy-done.7
  8.3 0.7 copy-done.8
  8.9 0.7 copy-done.9
  9.6 0.7 copy-done.10
  10.2 117.1 %layer_pair.1 = (bf16[512,2048]{1,0:T(8,128)(2,1)}, bf16[512,1024]{1,0:T(8,128)(2,1)}, bf16[1,32,64,256]{3,2,1,0:T(8,128)(2,1)}) custom-call(s32[32]{0:T(128)S(1)} %copy-done.7, s32[32]{0:T(128)S(1)} %copy-done.8, s32[32]{0:T(128)S(1)} %copy-done.9, s32[32]{0:T(128)S(1)} %select_reduce_fusion.sources, f32[32]{0:T(128)S(1)} %copy-done.10, ...), custom_call_target="tpu_custom_call" | custom-call | tf_op jit(solution)/shard_map/layer_pair/pallas_call | solution.py:431
  127.3 0.0 copy-start.12
  127.3 0.0 copy-start.11
  127.3 3.3 %copy.22 = bf16[512,2048]{1,0:T(8,128)(2,1)} copy(bf16[512,2048]{1,0:T(8,128)(2,1)} %get-tuple-element.6) | data formatting | bytes 4194304
  130.6 0.0 copy-done.12
  130.6 1.0 copy.23
  131.6 0.0 copy-done.11
  131.6 1.0 copy.24
  (7 shorter events, 0.0 us)
Async XLA Ops:
  1.4 1.0 copy-start
  2.4 0.9 copy-start.1
  3.3 0.9 copy-start.2
  4.3 0.9 copy-start.3
  5.2 0.9 copy-start.4
  6.1 0.8 copy-start.5
  6.9 0.7 copy-start.6
  7.6 0.7 copy-start.7
  8.3 0.7 copy-start.8
  8.9 0.7 copy-start.9
  9.6 0.7 copy-start.10
  127.3 3.3 %copy-start.12 = (bf16[512,1024]{1,0:T(8,128)(2,1)S(1)}, bf16[512,1024]{1,0:T(8,128)(2,1)}, u32[]{:S(2)}) copy-start(bf16[512,1024]{1,0:T(8,128)(2,1)} %get-tuple-element.7) | copy-start | bytes 3145732
  127.3 4.3 %copy-start.11 = (bf16[1,32,64,256]{3,2,1,0:T(8,128)(2,1)S(1)}, bf16[1,32,64,256]{3,2,1,0:T(8,128)(2,1)}, u32[]{:S(2)}) copy-start(bf16[1,32,64,256]{3,2,1,0:T(8,128)(2,1)} %get-tuple-element.8) | copy-start | bytes 3145732
where the time goes:
time: 133 us
  Pallas kernels  117 us (88%)
  local copies, waits for them, and re-layouts  14.1 us (11%)
    pallas_call x1, Pallas kernels, local(): pl.pallas_call(kernel, out_shape=(jax.ShapeDtypeStruct((ROWS, HEADS * MDI...  117 us
    unnamed x29, local copies, waits for them, and re-layouts  14.1 us

commit v1 on v0

--- a/solution.py
+++ b/solution.py
@@ -34,13 +34,13 @@
 
 
 def kernel(
-    ids,
-    lengths,
-    holders,
-    sources,
-    rates,
-    steps,
-    gain,
+    ids_hbm,
+    lengths_hbm,
+    holders_hbm,
+    new_hbm,
+    rates_hbm,
+    steps_hbm,
+    gain_hbm,
     x_hbm,
     gate_hbm,
     write_hbm,
@@ -53,6 +53,14 @@
     ssm_out,
     attn_out,
     stored,
+    ids,
+    lengths,
+    holders,
+    new_holders,
+    sources,
+    rates,
+    steps,
+    gain,
     x_v,
     gate_v,
     write_v,
@@ -78,12 +86,9 @@
     cache_p,
     cache_b,
     final_p,
-    attn_v,
-    norm_v,
     square_mine,
     square_a,
     in_sem,
-    out_sem,
     own_sem,
     send_sem,
     recv_sem,
@@ -101,6 +106,13 @@
             (sk_hbm, sk_v),
             (sv_hbm, sv_v),
             (gate_hbm, gate_v),
+            (rates_hbm, rates),
+            (steps_hbm, steps),
+            (ids_hbm, ids),
+            (lengths_hbm, lengths),
+            (holders_hbm, holders),
+            (new_hbm, new_holders),
+            (gain_hbm, gain),
         )
     ):
         loads.append(pltpu.make_async_copy(src, dst, in_sem.at[n]))
@@ -122,6 +134,9 @@
 
     lax.fori_loop(1, SLOTS, greet_member, 0)
     lax.fori_loop(1, RANKS, greet_rank, 0)
+
+    loads[7].wait()
+    loads[8].wait()
 
     def head_logs(h, carry):
         row = pl.ds(h, 1)
@@ -186,6 +201,18 @@
     own_held = pltpu.make_async_copy(held.at[0, me], held_a.at[me], own_sem.at[1])
     own_cache.start()
     own_held.start()
+
+    for n in range(9, 14):
+        loads[n].wait()
+
+    def find_source(d, carry):
+        source = 0
+        for r in range(1, SLOTS):
+            source = jnp.where(new_holders[r] == d, r, source)
+        sources[d] = source
+        return carry
+
+    lax.fori_loop(0, SLOTS, find_source, 0)
 
     loads[0].wait()
     loads[1].wait()
@@ -317,12 +344,10 @@
             own = jnp.exp(own - highest)
             totals = jnp.sum(prefix, axis=1, keepdims=True) + jnp.sum(own, axis=1, keepdims=True)
             mixed = dot(prefix.astype(BF16), prefix_values) + dot(own.astype(BF16), sv_v[:width, :])
-            attn_v[rows, head] = (mixed / totals).astype(BF16)
+            attn_out[rows, head] = (mixed / totals).astype(BF16)
         return carry
 
     lax.fori_loop(0, QH, attend, 0)
-    attn_store = pltpu.make_async_copy(attn_v, attn_out, out_sem.at[0])
-    attn_store.start()
 
     arrived(local_a, 2)
     arrived(total_a, 3)
@@ -381,15 +406,11 @@
 
     def norm(j, carry):
         pair = pl.ds(pl.multiple_of(j * 128, 128), 128)
-        norm_v[:, pair] = (y_v[j] * inverse * gain[pl.ds(j, 1), :]).astype(BF16)
+        ssm_out[:, pair] = (y_v[j] * inverse * gain[pl.ds(j, 1), :]).astype(BF16)
         return carry
 
     lax.fori_loop(0, PAIRS, norm, 0)
-    norm_store = pltpu.make_async_copy(norm_v, ssm_out, out_sem.at[1])
-    norm_store.start()
-
-    attn_store.wait()
-    norm_store.wait()
+
     own_final.wait()
     sent(cache_a, 0)
     sent(held_a, 1)
@@ -421,23 +442,27 @@
     holder_slots,
     new_holders,
 ):
-    slots = jnp.arange(SLOTS, dtype=jnp.int32)
-    sources = jnp.sum(jnp.where(new_holders[None, :] == slots[:, None], slots[None, :], 0), 1)
-    smem = pl.BlockSpec(memory_space=pltpu.SMEM)
-    vmem = pl.BlockSpec(memory_space=pltpu.VMEM)
-    anywhere = pl.BlockSpec(memory_space=pl.ANY)
+    hbm = pl.BlockSpec(memory_space=pltpu.HBM)
     state = (SLOTS, MDIM, STATE)
     cache = (SLOTS, 2, PIECE, HDIM)
-    return pl.pallas_call(
+    outs = pl.pallas_call(
         kernel,
         out_shape=(
-            jax.ShapeDtypeStruct((ROWS, HEADS * MDIM), BF16),
-            jax.ShapeDtypeStruct((ROWS, QH * HDIM), BF16),
-            jax.ShapeDtypeStruct((1,) + state, BF16),
+            pltpu.VMEM((ROWS, HEADS * MDIM), BF16),
+            pltpu.VMEM((ROWS, QH * HDIM), BF16),
+            pltpu.VMEM((1,) + state, BF16),
         ),
-        in_specs=[smem] * 5 + [vmem] * 2 + [anywhere] * 9,
-        out_specs=(anywhere,) * 3,
+        in_specs=[hbm] * 16,
+        out_specs=(pl.BlockSpec(memory_space=pltpu.VMEM),) * 3,
         scratch_shapes=[
+            pltpu.SMEM((SLOTS,), jnp.int32),
+            pltpu.SMEM((SLOTS,), jnp.int32),
+            pltpu.SMEM((SLOTS,), jnp.int32),
+            pltpu.SMEM((SLOTS,), jnp.int32),
+            pltpu.SMEM((SLOTS,), jnp.int32),
+            pltpu.SMEM((HEADS,), F32),
+            pltpu.VMEM((HEADS, ROWS), F32),
+            pltpu.VMEM((PAIRS, 128), F32),
             pltpu.VMEM((ROWS, HEADS * MDIM), BF16),
             pltpu.VMEM((ROWS, HEADS * MDIM), BF16),
             pltpu.VMEM((ROWS, STATE), BF16),
@@ -463,25 +488,22 @@
             pltpu.VMEM(cache, BF16),
             pltpu.VMEM(cache, BF16),
             pltpu.VMEM(state, BF16),
-            pltpu.VMEM((ROWS, QH * HDIM), BF16),
-            pltpu.VMEM((ROWS, HEADS * MDIM), BF16),
             pltpu.VMEM((1, ROWS), F32),
             pltpu.VMEM((RANKS, 1, ROWS), F32),
-            pltpu.SemaphoreType.DMA((7,)),
-            pltpu.SemaphoreType.DMA((2,)),
+            pltpu.SemaphoreType.DMA((14,)),
             pltpu.SemaphoreType.DMA((3,)),
             pltpu.SemaphoreType.DMA((8,)),
             pltpu.SemaphoreType.DMA((8,)),
         ],
         compiler_params=pltpu.CompilerParams(
-            collective_id=0, has_side_effects=True, vmem_limit_bytes=52 * 2**20
+            collective_id=0, has_side_effects=True, vmem_limit_bytes=44 * 2**20
         ),
         name="layer_pair",
-    )(
+    )(*(pltpu.with_memory_space_constraint(a, pltpu.HBM) for a in (
         prefix_ids,
         prefix_lengths,
         holder_slots,
-        sources,
+        new_holders,
         decay_rates,
         step_sizes,
         norm_gain.reshape(PAIRS, 128),
@@ -494,7 +516,34 @@
         suffix_values,
         held_state,
         held_cache,
-    )
+    )))
+    return pl.pallas_call(
+        hand_over,
+        out_shape=tuple(jax.ShapeDtypeStruct(out.shape, out.dtype) for out in outs),
+        in_specs=[pl.BlockSpec(memory_space=pltpu.VMEM)] * 3,
+        out_specs=(hbm,) * 3,
+        scratch_shapes=[pltpu.SemaphoreType.DMA((8,))],
+        compiler_params=pltpu.CompilerParams(vmem_limit_bytes=2**20),
+        name="hand_over",
+    )(*outs)
+
+
+def hand_over(ssm, attn, state, ssm_out, attn_out, stored, sem):
+    copies = []
+    for n in range(4):
+        rows = pl.ds(n * 128, 128)
+        copies.append((ssm.at[rows], ssm_out.at[rows]))
+    for n in range(2):
+        rows = pl.ds(n * 256, 256)
+        copies.append((attn.at[rows], attn_out.at[rows]))
+    for n in range(2):
+        heads = pl.ds(n * 16, 16)
+        copies.append((state.at[0, heads], stored.at[0, heads]))
+    copies = [pltpu.make_async_copy(a, b, sem.at[n]) for n, (a, b) in enumerate(copies)]
+    for c in copies:
+        c.start()
+    for c in copies:
+        c.wait()
 
 
 def solution(mesh):

time: 133 us -> 119 us (0.89)
  local copies, waits for them, and re-layouts: 14.1 us -> 0 us
  Pallas kernels: 117 us -> 119 us
    unnamed x29 -> x0, local copies, waits for them, and re-layouts: 14.1 us -> none
    pallas_call x1 -> x2, Pallas kernels: 117 us -> 119 us  [the longest x1 116 us: local(): pl.pallas_call(kernel, out_shape=(pltpu.VMEM((ROWS, HEADS * MDIM), BF16),...]
where the time goes in v1:
time: 119 us
  Pallas kernels  119 us (100%)
    pallas_call x1, Pallas kernels, local(): pl.pallas_call(kernel, out_shape=(pltpu.VMEM((ROWS, HEADS * MDIM), BF16),...  116 us

profile of v1, /device:TPU:1, one launch (start us, length us, event | category | flops | bytes accessed | tf_op | source)
XLA Modules:
  0.0 119.2 jit_solution(8630055668454370503)
XLA Ops:
  0.6 116.4 %layer_pair.1 = (bf16[512,2048]{1,0:T(8,128)(2,1)S(1)}, bf16[512,1024]{1,0:T(8,128)(2,1)S(1)}, bf16[1,32,64,256]{3,2,1,0:T(8,128)(2,1)S(1)}) custom-call(s32[32]{0:T(128)} %ids_hbm.1, s32[32]{0:T(128)} %lengths_hbm.1, s32[32]{0:T(128)} %holders_hbm.1, s32[32]{0:T(128)} %new_hbm.1, f32[32]{0:T(128)} %rates_hbm.1, f32[32,512]{1,0:T(8,128)} %steps_hbm.1, ...), custom_call_target="tpu_custom_call" | custom-call | tf_op jit(solution)/shard_map/layer_pair/pallas_call | solution.py:448
  117.1 2.1 %hand_over.1 = (bf16[512,2048]{1,0:T(8,128)(2,1)}, bf16[512,1024]{1,0:T(8,128)(2,1)}, bf16[1,32,64,256]{3,2,1,0:T(8,128)(2,1)}) custom-call(bf16[512,2048]{1,0:T(8,128)(2,1)S(1)} %get-tuple-element.6.ssm, bf16[512,1024]{1,0:T(8,128)(2,1)S(1)} %get-tuple-element.7.attn, bf16[1,32,64,256]{3,2,1,0:T(8,128)(2,1)S(1)} %get-tuple-element.8.state), custom_call_target="tpu_custom_call" | custom-call | tf_op jit(solution)/shard_map/hand_over/pallas_call | solution.py:520

commit v2 on v1

--- a/solution.py
+++ b/solution.py
@@ -96,6 +96,23 @@
     me = lax.axis_index("group")
     rank = lax.axis_index("tensor")
 
+    barrier = pltpu.get_barrier_semaphore()
+
+    def greet_member(k, carry):
+        pl.semaphore_signal(
+            barrier, inc=1, device_id={"group": lax.rem(me + k, SLOTS)}, device_id_type=MESH
+        )
+        return carry
+
+    def greet_rank(k, carry):
+        pl.semaphore_signal(
+            barrier, inc=1, device_id={"tensor": lax.rem(rank + k, RANKS)}, device_id_type=MESH
+        )
+        return carry
+
+    lax.fori_loop(1, SLOTS, greet_member, 0)
+    lax.fori_loop(1, RANKS, greet_rank, 0)
+
     loads = []
     for n, (src, dst) in enumerate(
         (
@@ -118,22 +135,61 @@
         loads.append(pltpu.make_async_copy(src, dst, in_sem.at[n]))
         loads[-1].start()
 
-    barrier = pltpu.get_barrier_semaphore()
-
-    def greet_member(k, carry):
-        pl.semaphore_signal(
-            barrier, inc=1, device_id={"group": lax.rem(me + k, SLOTS)}, device_id_type=MESH
+    pl.semaphore_wait(barrier, SLOTS - 1 + RANKS - 1)
+
+    def to_member(p, src, dst, n):
+        return pltpu.make_async_remote_copy(
+            src_ref=src,
+            dst_ref=dst,
+            send_sem=send_sem.at[n],
+            recv_sem=recv_sem.at[n],
+            device_id={"group": p},
+            device_id_type=MESH,
         )
-        return carry
-
-    def greet_rank(k, carry):
-        pl.semaphore_signal(
-            barrier, inc=1, device_id={"tensor": lax.rem(rank + k, RANKS)}, device_id_type=MESH
-        )
-        return carry
-
-    lax.fori_loop(1, SLOTS, greet_member, 0)
-    lax.fori_loop(1, RANKS, greet_rank, 0)
+
+    def arrived(buf, n, count=SLOTS - 1):
+        part = buf.at[pl.ds(0, count)]
+        pltpu.make_async_copy(part, part, recv_sem.at[n]).wait()
+
+    def sent(buf, n, count=SLOTS - 1):
+        part = buf.at[pl.ds(0, count)]
+        pltpu.make_async_copy(part, part, send_sem.at[n]).wait()
+
+    turn = lax.rem(me, 2) + 2 * (me // 16)
+
+    def in_order(zs, send):
+        for z in zs:
+            def one(k, carry, z=z):
+                at = lax.rem(k + turn, 4)
+                p = lax.rem(at, 2) + 2 * z + 16 * (at // 2)
+
+                @pl.when(p != me)
+                def _():
+                    send(p)
+
+                return carry
+
+            lax.fori_loop(0, 4, one, 0)
+
+    def cache_rows(p):
+        return cache.at[0, :, pl.ds(pl.multiple_of(p * PIECE, PIECE), PIECE), :]
+
+    def spread_cache(k, carry):
+        p = lax.rem(me + k, SLOTS)
+        to_member(p, cache_rows(p), cache_a.at[me], 0).start()
+        return carry
+
+    def spread_held(k, carry):
+        p = lax.rem(me + k, SLOTS)
+        to_member(p, held.at[0, p], held_a.at[me], 1).start()
+        return carry
+
+    lax.fori_loop(1, SLOTS, spread_cache, 0)
+    lax.fori_loop(1, SLOTS, spread_held, 0)
+    own_cache = pltpu.make_async_copy(cache_rows(me), cache_a.at[me], own_sem.at[0])
+    own_held = pltpu.make_async_copy(held.at[0, me], held_a.at[me], own_sem.at[1])
+    own_cache.start()
+    own_held.start()
 
     loads[7].wait()
     loads[8].wait()
@@ -162,46 +218,6 @@
         HEADS, 1, 128
     )
 
-    pl.semaphore_wait(barrier, SLOTS - 1 + RANKS - 1)
-
-    def to_member(p, src, dst, n):
-        return pltpu.make_async_remote_copy(
-            src_ref=src,
-            dst_ref=dst,
-            send_sem=send_sem.at[n],
-            recv_sem=recv_sem.at[n],
-            device_id={"group": p},
-            device_id_type=MESH,
-        )
-
-    def arrived(buf, n, count=SLOTS - 1):
-        part = buf.at[pl.ds(0, count)]
-        pltpu.make_async_copy(part, part, recv_sem.at[n]).wait()
-
-    def sent(buf, n, count=SLOTS - 1):
-        part = buf.at[pl.ds(0, count)]
-        pltpu.make_async_copy(part, part, send_sem.at[n]).wait()
-
-    def cache_rows(p):
-        return cache.at[0, :, pl.ds(pl.multiple_of(p * PIECE, PIECE), PIECE), :]
-
-    def spread_cache(k, carry):
-        p = lax.rem(me + k, SLOTS)
-        to_member(p, cache_rows(p), cache_a.at[me], 0).start()
-        return carry
-
-    def spread_held(k, carry):
-        p = lax.rem(me + k, SLOTS)
-        to_member(p, held.at[0, p], held_a.at[me], 1).start()
-        return carry
-
-    lax.fori_loop(1, SLOTS, spread_cache, 0)
-    lax.fori_loop(1, SLOTS, spread_held, 0)
-    own_cache = pltpu.make_async_copy(cache_rows(me), cache_a.at[me], own_sem.at[0])
-    own_held = pltpu.make_async_copy(held.at[0, me], held_a.at[me], own_sem.at[1])
-    own_cache.start()
-    own_held.start()
-
     for n in range(9, 14):
         loads[n].wait()
 
@@ -222,9 +238,12 @@
         a, b = pl.ds(2 * j, 1), pl.ds(2 * j + 1, 1)
         pair = pl.ds(pl.multiple_of(j * 128, 128), 128)
         turned = jnp.transpose(x_v[:, pair].astype(F32))
-        scaled = (turned * jnp.where(first_row, scale_v[a, :], scale_v[b, :])).astype(BF16)
-        entry = dot(scaled[:, :BLOCK], write_v[:BLOCK, :])
-        later = dot(scaled[:, BLOCK:], write_v[BLOCK:, :])
+        scaled = turned * jnp.where(first_row, scale_v[a, :], scale_v[b, :])
+        high = scaled.astype(BF16)
+        low = (scaled - high.astype(F32)).astype(BF16)
+        early, late = write_v[:BLOCK, :], write_v[BLOCK:, :]
+        entry = dot(high[:, :BLOCK], early) + dot(low[:, :BLOCK], early)
+        later = dot(high[:, BLOCK:], late) + dot(low[:, BLOCK:], late)
         entry_v[j] = entry.astype(BF16)
         fade = jnp.where(first_row, fade_v[a, :], fade_v[b, :])
         local_mine[pl.ds(2 * j, 2)] = (
@@ -362,12 +381,7 @@
 
     lax.fori_loop(0, SLOTS, pick_final, 0)
 
-    def store_final(k, carry):
-        p = lax.rem(me + k, SLOTS)
-        to_member(p, final_p.at[p], stored.at[0, me], 6).start()
-        return carry
-
-    lax.fori_loop(1, SLOTS, store_final, 0)
+    in_order((0, 1, 2, 3, 7, 4, 6, 5), lambda p: to_member(p, final_p.at[p], stored.at[0, me], 6).start())
     own_final = pltpu.make_async_copy(final_p.at[me], stored.at[0, me], own_sem.at[2])
     own_final.start()
 

time: 119 us -> 116 us (0.975)
  Pallas kernels: 119 us -> 115 us
    pallas_call x1, Pallas kernels: 116 us -> 113 us  [local(): pl.pallas_call(kernel, out_shape=(pltpu.VMEM((ROWS, HEADS * MDIM), BF16),...]
where the time goes in v2:
time: 116 us
  Pallas kernels  115 us (99%)
    pallas_call x1, Pallas kernels, local(): pl.pallas_call(kernel, out_shape=(pltpu.VMEM((ROWS, HEADS * MDIM), BF16),...  113 us

profile of v2, /device:TPU:1, one launch (start us, length us, event | category | flops | bytes accessed | tf_op | source)
XLA Modules:
  0.0 115.9 jit_solution(6545170587940744434)
XLA Ops:
  0.6 113.1 %layer_pair.1 = (bf16[512,2048]{1,0:T(8,128)(2,1)S(1)}, bf16[512,1024]{1,0:T(8,128)(2,1)S(1)}, bf16[1,32,64,256]{3,2,1,0:T(8,128)(2,1)S(1)}) custom-call(s32[32]{0:T(128)} %ids_hbm.1, s32[32]{0:T(128)} %lengths_hbm.1, s32[32]{0:T(128)} %holders_hbm.1, s32[32]{0:T(128)} %new_hbm.1, f32[32]{0:T(128)} %rates_hbm.1, f32[32,512]{1,0:T(8,128)} %steps_hbm.1, ...), custom_call_target="tpu_custom_call" | custom-call | tf_op jit(solution)/shard_map/layer_pair/pallas_call | solution.py:462
  113.8 2.1 %hand_over.1 = (bf16[512,2048]{1,0:T(8,128)(2,1)}, bf16[512,1024]{1,0:T(8,128)(2,1)}, bf16[1,32,64,256]{3,2,1,0:T(8,128)(2,1)}) custom-call(bf16[512,2048]{1,0:T(8,128)(2,1)S(1)} %get-tuple-element.6.ssm, bf16[512,1024]{1,0:T(8,128)(2,1)S(1)} %get-tuple-element.7.attn, bf16[1,32,64,256]{3,2,1,0:T(8,128)(2,1)S(1)} %get-tuple-element.8.state), custom_call_target="tpu_custom_call" | custom-call | tf_op jit(solution)/shard_map/hand_over/pallas_call | solution.py:534

commit v3 on v2

--- a/solution.py
+++ b/solution.py
@@ -218,6 +218,14 @@
         HEADS, 1, 128
     )
 
+    def spread_total(k, carry):
+        p = lax.rem(me + k, SLOTS)
+        to_member(p, total_mine.at[p], total_a.at[me], 3).start()
+        return carry
+
+    lax.fori_loop(1, SLOTS, spread_total, 0)
+    total_a[me] = total_mine[me]
+
     for n in range(9, 14):
         loads[n].wait()
 
@@ -256,12 +264,10 @@
     def spread_local(k, carry):
         p = lax.rem(me + k, SLOTS)
         to_member(p, local_mine.at[p], local_a.at[me], 2).start()
-        to_member(p, total_mine.at[p], total_a.at[me], 3).start()
         return carry
 
     lax.fori_loop(1, SLOTS, spread_local, 0)
     local_a[me] = local_mine[me]
-    total_a[me] = total_mine[me]
 
     own_cache.wait()
     arrived(cache_a, 0)
@@ -381,7 +387,18 @@
 
     lax.fori_loop(0, SLOTS, pick_final, 0)
 
-    in_order((0, 1, 2, 3, 7, 4, 6, 5), lambda p: to_member(p, final_p.at[p], stored.at[0, me], 6).start())
+    in_order((0,), lambda p: to_member(p, final_p.at[p], stored.at[0, me], 6).start())
+
+    def store_final(k, carry):
+        p = lax.rem(me + k, SLOTS)
+
+        @pl.when(lax.rem(p // 2, 8) >= 1)
+        def _():
+            to_member(p, final_p.at[p], stored.at[0, me], 6).start()
+
+        return carry
+
+    lax.fori_loop(1, SLOTS, store_final, 0)
     own_final = pltpu.make_async_copy(final_p.at[me], stored.at[0, me], own_sem.at[2])
     own_final.start()
 

time: 116 us -> 116 us (level)
  the two profiles are of different devices: /device:TPU:1 before, /device:TPU:65 now
where the time goes in v3:
time: 116 us
  Pallas kernels  116 us (100%)
    pallas_call x1, Pallas kernels, local(): pl.pallas_call(kernel, out_shape=(pltpu.VMEM((ROWS, HEADS * MDIM), BF16),...  114 us

profile of v3, /device:TPU:65, one launch (start us, length us, event | category | flops | bytes accessed | tf_op | source)
XLA Modules:
  0.0 116.4 jit_solution(17629753249644780491)
XLA Ops:
  0.6 113.6 %layer_pair.1 = (bf16[512,2048]{1,0:T(8,128)(2,1)S(1)}, bf16[512,1024]{1,0:T(8,128)(2,1)S(1)}, bf16[1,32,64,256]{3,2,1,0:T(8,128)(2,1)S(1)}) custom-call(s32[32]{0:T(128)} %ids_hbm.1, s32[32]{0:T(128)} %lengths_hbm.1, s32[32]{0:T(128)} %holders_hbm.1, s32[32]{0:T(128)} %new_hbm.1, f32[32]{0:T(128)} %rates_hbm.1, f32[32,512]{1,0:T(8,128)} %steps_hbm.1, ...), custom_call_target="tpu_custom_call" | custom-call | tf_op jit(solution)/shard_map/layer_pair/pallas_call | solution.py:479
  114.3 2.1 %hand_over.1 = (bf16[512,2048]{1,0:T(8,128)(2,1)}, bf16[512,1024]{1,0:T(8,128)(2,1)}, bf16[1,32,64,256]{3,2,1,0:T(8,128)(2,1)}) custom-call(bf16[512,2048]{1,0:T(8,128)(2,1)S(1)} %get-tuple-element.6.ssm, bf16[512,1024]{1,0:T(8,128)(2,1)S(1)} %get-tuple-element.7.attn, bf16[1,32,64,256]{3,2,1,0:T(8,128)(2,1)S(1)} %get-tuple-element.8.state), custom_call_target="tpu_custom_call" | custom-call | tf_op jit(solution)/shard_map/hand_over/pallas_call | solution.py:551
